TPU v7x, 32 devices: a whole 2x2x4 slice. The times are simulated.
32 devices in a mesh: dp: 4 (over z), ctx: 8 (over y, x, core).
Axes of the slice: x: 2, y: 2, z: 4, core: 2. Of those that a mesh axis runs over, the one named last changes fastest.
Arguments:
- hyena_q: bfloat16 [4, 1024, 4096], P('dp', 'ctx'), may hold values from -6 to 6
- hyena_k: bfloat16 [4, 1024, 4096], P('dp', 'ctx'), may hold values from -6 to 6
- hyena_v: bfloat16 [4, 1024, 4096], P('dp', 'ctx'), may hold values from -6 to 6
- hyena_cot: bfloat16 [4, 1024, 4096], P('dp', 'ctx'), may hold values from -6 to 6
- doc_lengths: int32 [4, 4], P('dp'), may hold values from 1 to 512, 1024 in all within a row
- decay_rate: float32 [16, 4096], P(None, ('dp', 'ctx')), may hold values from 0.00048828125 to 0.05
- residues: float32 [16, 4096], P(None, ('dp', 'ctx')), may hold values from -0.12 to 0.12
- skip_gain: float32 [4096], P(('dp', 'ctx')), may hold values from -3 to 3
Outputs:
- hyena_out: bfloat16 [4, 1024, 4096], P('dp', 'ctx')
- grad_hyena_q: bfloat16 [4, 1024, 4096], P('dp', 'ctx')
- grad_hyena_k: bfloat16 [4, 1024, 4096], P('dp', 'ctx')
- grad_hyena_v: bfloat16 [4, 1024, 4096], P('dp', 'ctx')
- grad_rate: float32 [16, 4096], P(None, ('dp', 'ctx'))
- grad_residues: float32 [16, 4096], P(None, ('dp', 'ctx'))
- grad_skip: float32 [4096], P(('dp', 'ctx'))
Inputs may be any that keep to these rules, and one draw needn't show every extreme that they name: `doc_lengths`: each row holds the lengths of the 4 documents of one sequence in order; they sum to 1024 and the longest is exactly half of 1024.
All inputs are finite; a program needn't handle non-finite values.
Results may differ from a plain program's by a relative error of at most 0.001.
Values sent between devices are 32-bit elements; how exact they have to be, the bound alone decides.
A program may use at most 192 MiB of HBM per device.

v0:
```python
import functools

import jax
import jax.numpy as jnp
from jax import lax
from jax.experimental import pallas as pl
from jax.experimental.pallas import tpu as pltpu
from jax.sharding import PartitionSpec as P

LANES = 128
ROWS = 8
GROUP = LANES * ROWS
HALF = 8
PAD = 8


def load_products(k_ref, v_ref, c_ref, q_ref, drive, pull, pitch):
    tokens = k_ref.shape[0]
    for i in range(ROWS):
        cols = pl.ds(i * LANES, LANES)
        rows = pl.ds(i * pitch, tokens)
        drive[rows, :] = k_ref[:, cols].astype(jnp.float32) * v_ref[:, cols].astype(jnp.float32)
        pull[rows, :] = c_ref[:, cols].astype(jnp.float32) * q_ref[:, cols].astype(jnp.float32)


def ends_kernel(keep_ref, flag_ref, par_ref, k_ref, v_ref, c_ref, q_ref, out_ref, drive, pull, *, modes, pitch):
    tokens = k_ref.shape[0]
    blocks = tokens // ROWS
    width = 2 * modes + 1
    base = pl.program_id(0) * ROWS * width
    load_products(k_ref, v_ref, c_ref, q_ref, drive, pull, pitch)
    lam = [jnp.exp(-par_ref[pl.ds(base + m, ROWS, stride=width), :]) for m in range(modes)]

    def steps(b, carry, masked):
        tails, heads = list(carry[0]), list(carry[1])
        for j in range(ROWS):
            t = b * ROWS + j
            u = tokens - 1 - t
            d = drive[pl.ds(t, ROWS, stride=pitch), :]
            p = pull[pl.ds(u, ROWS, stride=pitch), :]
            for m in range(modes):
                if masked:
                    tails[m] = lam[m] * keep_ref[t] * tails[m] + d
                    heads[m] = lam[m] * keep_ref[u] * (heads[m] + p)
                else:
                    tails[m] = lam[m] * tails[m] + d
                    heads[m] = lam[m] * (heads[m] + p)
        return tuple(tails), tuple(heads)

    def body(b, carry):
        broken = flag_ref[b] + flag_ref[blocks - 1 - b] > 0
        return lax.cond(broken, lambda c: steps(b, c, True), lambda c: steps(b, c, False), carry)

    zeros = tuple(jnp.zeros((ROWS, LANES), jnp.float32) for _ in range(modes))
    tails, heads = lax.fori_loop(0, blocks, body, (zeros, zeros))
    for m in range(modes):
        out_ref[m] = tails[m]
        out_ref[modes + m] = heads[m]


def main_kernel(
    keep_ref, flag_ref, par_ref, in_ref, k_ref, v_ref, c_ref, q_ref,
    out_ref, gq_ref, gk_ref, gv_ref, grad_ref,
    drive, pull, filt, gdrive, states, *, modes, pitch,
):
    tokens = k_ref.shape[0]
    blocks = tokens // ROWS
    width = 2 * modes + 1
    base = pl.program_id(0) * ROWS * width
    load_products(k_ref, v_ref, c_ref, q_ref, drive, pull, pitch)
    skip = par_ref[pl.ds(base + 2 * modes, ROWS, stride=width), :]
    skip_sum = jnp.zeros((ROWS, LANES), jnp.float32)

    for first in range(0, modes, HALF):
        lam = [jnp.exp(-par_ref[pl.ds(base + first + m, ROWS, stride=width), :]) for m in range(HALF)]
        res = [par_ref[pl.ds(base + modes + first + m, ROWS, stride=width), :] for m in range(HALF)]
        start = tuple(in_ref[first + m] for m in range(HALF))
        for m in range(HALF):
            states[0, m] = start[m]

        def forward(b, carry, masked):
            x, sums, skips = list(carry[0]), list(carry[1]), carry[2]
            for j in range(ROWS):
                t = b * ROWS + j
                here = pl.ds(t, ROWS, stride=pitch)
                d = drive[here, :]
                p = pull[here, :]
                if first == 0:
                    total = skip * d
                    skips = skips + p * d
                else:
                    total = filt[here, :]
                for m in range(HALF):
                    if masked:
                        x[m] = lam[m] * keep_ref[t] * x[m] + d
                    else:
                        x[m] = lam[m] * x[m] + d
                    states[t + 1, m] = x[m]
                    sums[m] = sums[m] + p * x[m]
                    total = total + res[m] * x[m]
                filt[here, :] = total
            return tuple(x), tuple(sums), skips

        def backward(b, carry, masked):
            inc, sums = list(carry[0]), list(carry[1])
            for j in reversed(range(ROWS)):
                t = b * ROWS + j
                here = pl.ds(t, ROWS, stride=pitch)
                p = pull[here, :]
                total = skip * p if first == 0 else gdrive[here, :]
                for m in range(HALF):
                    a = p + inc[m]
                    total = total + res[m] * a
                    inc[m] = lam[m] * keep_ref[t] * a if masked else lam[m] * a
                    sums[m] = sums[m] + inc[m] * states[t, m]
                gdrive[here, :] = total
            return tuple(inc), tuple(sums)

        def forward_body(b, carry):
            return lax.cond(
                flag_ref[b] > 0, lambda c: forward(b, c, True), lambda c: forward(b, c, False), carry
            )

        def backward_body(i, carry):
            b = blocks - 1 - i
            return lax.cond(
                flag_ref[b] > 0, lambda c: backward(b, c, True), lambda c: backward(b, c, False), carry
            )

        zeros = tuple(jnp.zeros((ROWS, LANES), jnp.float32) for _ in range(HALF))
        _, sums, skip_sum = lax.fori_loop(0, blocks, forward_body, (start, zeros, skip_sum))
        for m in range(HALF):
            grad_ref[modes + first + m] = sums[m]
        incoming = tuple(in_ref[modes + first + m] for m in range(HALF))
        _, sums = lax.fori_loop(0, blocks, backward_body, (incoming, zeros))
        for m in range(HALF):
            grad_ref[first + m] = -res[m] * sums[m]
    grad_ref[2 * modes] = skip_sum

    for i in range(ROWS):
        cols = pl.ds(i * LANES, LANES)
        rows = pl.ds(i * pitch, tokens)
        f = filt[rows, :]
        g = gdrive[rows, :]
        out_ref[:, cols] = (q_ref[:, cols].astype(jnp.float32) * f).astype(jnp.bfloat16)
        gq_ref[:, cols] = (c_ref[:, cols].astype(jnp.float32) * f).astype(jnp.bfloat16)
        gk_ref[:, cols] = (g * v_ref[:, cols].astype(jnp.float32)).astype(jnp.bfloat16)
        gv_ref[:, cols] = (g * k_ref[:, cols].astype(jnp.float32)).astype(jnp.bfloat16)


def join_kernel(weight_ref, par_ref, all_ref, out_ref, *, modes, tokens):
    count = all_ref.shape[0]
    mine = lax.axis_index("ctx")
    width = 2 * modes + 1
    base = pl.program_id(0) * ROWS * width
    for m in range(modes):
        across = jnp.exp(-float(tokens) * par_ref[pl.ds(base + m, ROWS, stride=width), :])

        def turn(i, carry):
            state, adjoint = carry
            j = count - 1 - i
            near = across * weight_ref[i] * state + all_ref[i, m]
            far = across * weight_ref[j] * adjoint + all_ref[j, modes + m]
            state = jnp.where(i < mine, near, state)
            adjoint = jnp.where(j > mine, far, adjoint)
            return state, adjoint

        zero = jnp.zeros((ROWS, LANES), jnp.float32)
        state, adjoint = lax.fori_loop(0, count, turn, (zero, zero), unroll=8)
        out_ref[m] = state
        out_ref[modes + m] = adjoint


def per_device(hyena_q, hyena_k, hyena_v, hyena_cot, doc_lengths, decay_rate, residues, skip_gain):
    tokens, channels = hyena_q.shape[1], hyena_q.shape[2]
    modes, own = decay_rate.shape
    width = 2 * modes + 1
    tiles = channels // LANES
    groups = channels // GROUP
    blocks = tokens // ROWS
    pitch = tokens + PAD
    count, mine = lax.axis_size("ctx"), lax.axis_index("ctx")
    axes = ("dp", "ctx")

    packed = jnp.concatenate([decay_rate, residues, skip_gain[None, :]], axis=0)
    params = lax.all_gather(packed, axes, axis=0)
    if own != LANES:
        params = params.transpose(1, 0, 2).reshape(width, tiles, LANES).transpose(1, 0, 2)
    params = params.reshape(tiles * width, LANES)

    lengths = doc_lengths[0]
    starts = (jnp.cumsum(lengths) - lengths)[1:]
    position = mine * tokens + jnp.arange(tokens, dtype=jnp.int32)
    starting = jnp.any(position[:, None] == starts[None, :], axis=1)
    keep = jnp.where(starting, 0.0, 1.0).astype(jnp.float32)
    flags = jnp.any(starting.reshape(blocks, ROWS), axis=1).astype(jnp.int32)
    place = jnp.arange(count)
    closed = jnp.any((starts // tokens)[None, :] == place[:, None], axis=1)
    opened = 1.0 - closed.astype(jnp.float32)
    weights = opened
    q, k, v, c = hyena_q[0], hyena_k[0], hyena_v[0], hyena_cot[0]

    smem = pl.BlockSpec(memory_space=pltpu.SMEM)
    whole = pl.BlockSpec((tiles * width, LANES), lambda g: (0, 0))
    block = pl.BlockSpec((tokens, GROUP), lambda g: (0, g))
    wide = pltpu.VMEM((ROWS * pitch, LANES), jnp.float32)
    limit = pltpu.CompilerParams(vmem_limit_bytes=48 * 1024 * 1024)

    def rows_of(n):
        return pl.BlockSpec((n, ROWS, LANES), lambda g: (0, g, 0))

    ends = pl.pallas_call(
        functools.partial(ends_kernel, modes=modes, pitch=pitch),
        grid=(groups,),
        in_specs=[smem, smem, whole, block, block, block, block],
        out_specs=rows_of(2 * modes),
        out_shape=jax.ShapeDtypeStruct((2 * modes, tiles, LANES), jnp.float32),
        scratch_shapes=[wide, wide],
        compiler_params=limit,
        name="ends",
    )(keep, flags, params, k, v, c, q)
    everyone = lax.all_gather(ends, "ctx", axis=0)
    incoming = pl.pallas_call(
        functools.partial(join_kernel, modes=modes, tokens=tokens),
        grid=(groups,),
        in_specs=[smem, whole, pl.BlockSpec((count, 2 * modes, ROWS, LANES), lambda g: (0, 0, g, 0))],
        out_specs=rows_of(2 * modes),
        out_shape=jax.ShapeDtypeStruct((2 * modes, tiles, LANES), jnp.float32),
        compiler_params=limit,
        name="join",
    )(weights, params, everyone)
    big = jax.ShapeDtypeStruct((tokens, channels), jnp.bfloat16)
    hyena_out, grad_q, grad_k, grad_v, grads = pl.pallas_call(
        functools.partial(main_kernel, modes=modes, pitch=pitch),
        grid=(groups,),
        in_specs=[smem, smem, whole, rows_of(2 * modes), block, block, block, block],
        out_specs=[block, block, block, block, rows_of(width)],
        out_shape=[big, big, big, big, jax.ShapeDtypeStruct((width, tiles, LANES), jnp.float32)],
        scratch_shapes=[wide, wide, wide, wide, pltpu.VMEM((tokens + 1, HALF, ROWS, LANES), jnp.float32)],
        compiler_params=limit,
        name="main",
    )(keep, flags, params, incoming, k, v, c, q)
    if own == LANES:
        shared = lax.psum_scatter(grads, axes, scatter_dimension=1, tiled=True).reshape(width, own)
    else:
        shared = lax.psum_scatter(grads.reshape(width, channels), axes, scatter_dimension=1, tiled=True)
    return (
        hyena_out[None], grad_q[None], grad_k[None], grad_v[None],
        shared[:modes], shared[modes : 2 * modes], shared[2 * modes],
    )


def solution(mesh):
    tokens_split = P("dp", "ctx", None)
    by_channel = P(None, ("dp", "ctx"))
    return jax.shard_map(
        per_device,
        mesh=mesh,
        in_specs=(tokens_split,) * 4 + (P("dp", None), by_channel, by_channel, P(("dp", "ctx"))),
        out_specs=(tokens_split,) * 4 + (by_channel, by_channel, P(("dp", "ctx"))),
        check_vma=False,
    )
```

profile of v0, /device:TPU:0, one launch (start us, length us, event | category | flops | bytes accessed | tf_op | source)
XLA Modules:
  0.0 264.3 jit_solution(8325161066236323652)
XLA Ops:
  7.2 0.0 all-gather.5.cloned.1.call-start
  7.2 0.8 reduce-window.9
  8.0 0.7 bitcast_subtract_fusion
  8.7 0.1 and_select_fusion
  8.8 0.1 compare_reduce_fusion
  8.9 0.1 reshape.60
  9.0 0.1 reduce_or.28
  9.1 0.7 maximum_bitcast_fusion
  9.8 45.0 %all-gather.2 = f32[32,33,128]{2,1,0:T(8,128)S(1)} all-gather(f32[1,33,128]{2,1,0:T(8,128)S(1)} %maximum_bitcast_fusion), channel_id=2, replica_groups=mesh['dp'=4,'ctx'=8] {'dp','ctx'}, dimensions={0}, use_global_device_ids=true | all-gather | bytes 557568 | tf_op jit(solution)/shard_map/all_gather | solution.py:186
  54.9 0.0 copy-start.1
  54.9 1.2 copy-done.1
  56.1 0.0 copy-start.3
  56.1 1.2 copy-done.3
  57.3 0.0 copy-start.5
  57.3 1.2 copy-done.5
  58.5 0.0 copy-start.7
  58.5 1.2 copy-done.7
  59.8 0.0 copy-start.2
  59.8 0.0 copy-start.4
  59.8 8.4 %ends.1 = f32[32,32,128]{2,1,0:T(8,128)} custom-call(f32[128]{0:T(128)S(1)} %broadcast_select_fusion.keep_ref, s32[16]{0:T(128)S(1)} %convert_element_type.6.flag_ref, f32[1056,128]{1,0:T(8,128)S(1)} %reshape.66.par_ref, bf16[128,4096]{1,0:T(8,128)(2,1)S(1)} %bitcast.24, bf16[128,4096]{1,0:T(8,128)(2,1)S(1)} %bitcast.26, bf16[128,4096]{1,0:T(8,128)(2,1)S(1)} %bitcast.28, ...), custom_call_target="tpu_custom_call" | custom-call | tf_op jit(solution)/shard_map/ends/pallas_call | solution.py:212
  68.2 0.0 all-gather.5.cloned.1.call-update
  68.2 0.0 all-reduce.3.cloned.1.call-start
  68.3 0.1 fusion
  68.4 32.6 %all-gather.5.cloned.1.call-done = f32[256,32,128]{2,1,0:T(8,128)} async-done(((f32[32,32,128]{2,1,0:T(8,128)}), f32[256,32,128]{2,1,0:T(8,128)}) %all-gather.5.cloned.1.call-update) | async-done | bytes 4194320 | tf_op jit(solution)/shard_map/all_gather | solution.py:222
  101.0 0.0 copy-start
  101.0 2.2 copy-done
  103.2 0.0 copy-start.6
  103.2 0.0 copy-start.8
  103.2 1.7 join.1.in_ref
  104.8 0.0 copy-done.2
  104.9 0.0 copy-done.4
  104.9 0.0 copy-done.6
  104.9 0.0 copy-done.8
  104.9 23.4 %main.1 = (bf16[128,4096]{1,0:T(8,128)(2,1)}, bf16[128,4096]{1,0:T(8,128)(2,1)}, bf16[128,4096]{1,0:T(8,128)(2,1)}, bf16[128,4096]{1,0:T(8,128)(2,1)}, f32[33,32,128]{2,1,0:T(8,128)}) custom-call(f32[128]{0:T(128)S(1)} %broadcast_select_fusion.keep_ref, s32[16]{0:T(128)S(1)} %convert_element_type.6.flag_ref, f32[1056,128]{1,0:T(8,128)S(1)} %reshape.66.par_ref, ...), custom_call_target="tpu_custom_call" | custom-call | tf_op jit(solution)/shard_map/main/pallas_call | solution.py:233
  128.3 0.0 all-reduce.3.cloned.1.call-update
  128.3 126.5 %all-reduce.3.cloned.1.call-done = f32[33,32,128]{2,1,0:T(8,128)} async-done(((f32[33,32,128]{2,1,0:T(8,128)}), f32[33,32,128]{2,1,0:T(8,128)}) %all-reduce.3.cloned.1.call-update) | async-done | bytes 540688
  254.8 1.5 constant_dynamic-slice_fusion
  256.3 1.2 fusion.1
  (5 shorter events, 0.1 us)
Async XLA Ops:
  7.2 93.8 %all-gather.5.cloned.1.call-start = ((), (), s32[]{:S(2)}) async-start(), calls=%async_computation | async-start | bytes 4718592 | tf_op jit(solution)/shard_map/all_gather | solution.py:222
  54.9 1.2 copy-start.1
  56.1 1.2 copy-start.3
  57.3 1.2 copy-start.5
  58.5 1.2 copy-start.7
  59.8 45.1 %copy-start.2 = (bf16[1,128,4096]{2,1,0:T(8,128)(2,1)S(1)}, bf16[1,128,4096]{2,1,0:T(8,128)(2,1)}, u32[]{:S(2)}) copy-start(bf16[1,128,4096]{2,1,0:T(8,128)(2,1)} %param.9) | copy-start | bytes 3145732
  59.8 45.1 %copy-start.4 = (bf16[1,128,4096]{2,1,0:T(8,128)(2,1)S(1)}, bf16[1,128,4096]{2,1,0:T(8,128)(2,1)}, u32[]{:S(2)}) copy-start(bf16[1,128,4096]{2,1,0:T(8,128)(2,1)} %param.10) | copy-start | bytes 3145732
  68.2 186.6 %all-reduce.3.cloned.1.call-start = ((), (), s32[]{:S(2)}) async-start(), calls=%async_computation.1 | async-start | bytes 1081344
  101.0 2.2 copy-start
  103.2 1.7 copy-start.6
  103.2 1.7 copy-start.8
Sparse Core Ops, SparseCore 0:
  68.4 32.5 all-gather.4
  128.4 126.3 all-reduce.2
where the time goes:
time: 265 us; the launch traced here: 264 us
  waiting for transfers between devices  159 us (60%)
  blocking collectives  45 us (17%)
  Pallas kernels  33.5 us (13%)
  between operations  14.1 us (5%)
  local copies, waits for them, and re-layouts  9.91 us (4%)
    unnamed x3, waiting for transfers between devices  127 us
    all_gather x1, blocking collectives, per_device(): params = lax.all_gather(packed, axes, axis=0)  45 us
    all_gather x1, waiting for transfers between devices, per_device(): everyone = lax.all_gather(ends, 'ctx', axis=0)  32.6 us
    pallas_call x1, Pallas kernels, per_device(): pl.pallas_call(functools.partial(main_kernel, modes=modes, pitch=pitch),...  23.4 us
    pallas_call x1, Pallas kernels, per_device(): pl.pallas_call(functools.partial(ends_kernel, modes=modes, pitch=pitch),...  8.44 us
    unnamed x19, local copies, waits for them, and re-layouts  7.14 us
  transfers between devices with their start and end apart: 2, of which 2 were waited for; matrix products, arithmetic and copies ran while one was open for 0% of the time, Pallas kernels for 0%

commit v1 on v0

--- a/solution.py
+++ b/solution.py
@@ -12,6 +12,115 @@
 GROUP = LANES * ROWS
 HALF = 8
 PAD = 8
+WIDTH = 40
+VMEM_LIMIT = 56 * 1024 * 1024
+MESH = pl.DeviceIdType.MESH
+
+
+def tile_rows(group, row, stride):
+    return pl.ds(group * (ROWS * WIDTH if stride == WIDTH else WIDTH) + row, ROWS, stride=stride)
+
+
+def greet(peers):
+    barrier = pltpu.get_barrier_semaphore()
+    for peer in peers:
+        pl.semaphore_signal(barrier, inc=1, device_id=peer, device_id_type=MESH)
+    pl.semaphore_wait(barrier, len(peers))
+
+
+def others(axis, size):
+    mine = lax.axis_index(axis)
+    return [lax.rem(mine + step, size) for step in range(1, size)]
+
+
+def push(source, target, send, recv, device):
+    copy = pltpu.make_async_remote_copy(
+        src_ref=source, dst_ref=target, send_sem=send, recv_sem=recv, device_id=device, device_id_type=MESH
+    )
+    copy.start()
+    return copy
+
+
+def gather_kernel(own_ref, out_ref, send_z, recv_z, send_p, recv_p, *, planes, count):
+    zs, ps = others("dp", planes), others("ctx", count)
+    greet([{"dp": z} for z in zs] + [{"ctx": p} for p in ps])
+    bundle = pl.ds(pl.multiple_of(lax.axis_index("ctx") * planes * WIDTH, WIDTH), planes * WIDTH)
+    slot = pl.ds(
+        pl.multiple_of((lax.axis_index("ctx") * planes + lax.axis_index("dp")) * WIDTH, WIDTH), WIDTH
+    )
+    copies = [push(own_ref, out_ref.at[slot], send_z.at[i], recv_z.at[i], {"dp": z}) for i, z in enumerate(zs)]
+    out_ref[slot, :] = own_ref[...]
+    for copy in copies:
+        copy.wait()
+    copies = [
+        push(out_ref.at[bundle], out_ref.at[bundle], send_p.at[i], recv_p.at[i], {"ctx": p})
+        for i, p in enumerate(ps)
+    ]
+    for copy in copies:
+        copy.wait()
+
+
+def exchange_kernel(open_ref, par_ref, ends_ref, out_ref, land, back, send_a, recv_a, send_b, recv_b,
+                    *, planes, count, tokens):
+    mine = lax.axis_index("ctx")
+    ps = others("ctx", count)
+    greet([{"ctx": p} for p in ps])
+    copies = [
+        push(ends_ref.at[p], land.at[mine], send_a.at[i], recv_a.at[i], {"ctx": p}) for i, p in enumerate(ps)
+    ]
+    land[mine] = ends_ref[mine]
+    share = ends_ref.shape[1] // 2
+    across = []
+    for s in range(share):
+        for g in range(planes):
+            rates = par_ref[pl.ds(g * WIDTH + mine * share + s, ROWS, stride=planes * WIDTH), :]
+            across.append(jnp.exp(-float(tokens) * rates))
+    for copy in copies:
+        copy.wait()
+    for s in range(share):
+        for g in range(planes):
+            rows = pl.ds(g * ROWS, ROWS)
+            factor = across[s * planes + g]
+            state = jnp.zeros((ROWS, LANES), jnp.float32)
+            adjoint = state
+            for p in range(count):
+                n = count - 1 - p
+                back[p, s, rows, :] = state
+                back[n, share + s, rows, :] = adjoint
+                state = factor * open_ref[p] * state + land[p, s, rows, :]
+                adjoint = factor * open_ref[n] * adjoint + land[n, share + s, rows, :]
+    copies = [
+        push(back.at[p], out_ref.at[mine], send_b.at[i], recv_b.at[i], {"ctx": p}) for i, p in enumerate(ps)
+    ]
+    out_ref[mine] = back[mine]
+    for copy in copies:
+        copy.wait()
+
+
+def reduce_kernel(grad_ref, out_ref, land, bundle, land_z, send_p, recv_p, send_z, recv_z, *, planes, count):
+    zs, ps = others("dp", planes), others("ctx", count)
+    greet([{"dp": z} for z in zs] + [{"ctx": p} for p in ps])
+    mine, plane = lax.axis_index("ctx"), lax.axis_index("dp")
+    copies = [
+        push(grad_ref.at[p], land.at[i], send_p.at[i], recv_p.at[i], {"ctx": p}) for i, p in enumerate(ps)
+    ]
+    for copy in copies:
+        copy.wait()
+    for z in range(planes):
+        rows = pl.ds(z * WIDTH, WIDTH)
+        total = grad_ref[mine, rows, :]
+        for i in range(count - 1):
+            total = total + land[i, rows, :]
+        bundle[z] = total
+    copies = [
+        push(bundle.at[z], land_z.at[i], send_z.at[i], recv_z.at[i], {"dp": z}) for i, z in enumerate(zs)
+    ]
+    for copy in copies:
+        copy.wait()
+    total = bundle[plane]
+    for i in range(planes - 1):
+        total = total + land_z[i]
+    out_ref[...] = total
 
 
 def load_products(k_ref, v_ref, c_ref, q_ref, drive, pull, pitch):
@@ -23,13 +132,12 @@
         pull[rows, :] = c_ref[:, cols].astype(jnp.float32) * q_ref[:, cols].astype(jnp.float32)
 
 
-def ends_kernel(keep_ref, flag_ref, par_ref, k_ref, v_ref, c_ref, q_ref, out_ref, drive, pull, *, modes, pitch):
+def ends_kernel(keep_ref, flag_ref, par_ref, k_ref, v_ref, c_ref, q_ref, out_ref, drive, pull, *, modes, pitch, stride, share):
     tokens = k_ref.shape[0]
     blocks = tokens // ROWS
-    width = 2 * modes + 1
-    base = pl.program_id(0) * ROWS * width
+    group = pl.program_id(0)
     load_products(k_ref, v_ref, c_ref, q_ref, drive, pull, pitch)
-    lam = [jnp.exp(-par_ref[pl.ds(base + m, ROWS, stride=width), :]) for m in range(modes)]
+    lam = [jnp.exp(-par_ref[tile_rows(group, m, stride), :]) for m in range(modes)]
 
     def steps(b, carry, masked):
         tails, heads = list(carry[0]), list(carry[1])
@@ -54,27 +162,26 @@
     zeros = tuple(jnp.zeros((ROWS, LANES), jnp.float32) for _ in range(modes))
     tails, heads = lax.fori_loop(0, blocks, body, (zeros, zeros))
     for m in range(modes):
-        out_ref[m] = tails[m]
-        out_ref[modes + m] = heads[m]
+        out_ref[m // share, m % share] = tails[m]
+        out_ref[m // share, share + m % share] = heads[m]
 
 
 def main_kernel(
     keep_ref, flag_ref, par_ref, in_ref, k_ref, v_ref, c_ref, q_ref,
     out_ref, gq_ref, gk_ref, gv_ref, grad_ref,
-    drive, pull, filt, gdrive, states, *, modes, pitch,
+    drive, pull, filt, gdrive, states, *, modes, pitch, stride, share,
 ):
     tokens = k_ref.shape[0]
     blocks = tokens // ROWS
-    width = 2 * modes + 1
-    base = pl.program_id(0) * ROWS * width
+    group = pl.program_id(0)
     load_products(k_ref, v_ref, c_ref, q_ref, drive, pull, pitch)
-    skip = par_ref[pl.ds(base + 2 * modes, ROWS, stride=width), :]
+    skip = par_ref[tile_rows(group, 2 * modes, stride), :]
     skip_sum = jnp.zeros((ROWS, LANES), jnp.float32)
 
     for first in range(0, modes, HALF):
-        lam = [jnp.exp(-par_ref[pl.ds(base + first + m, ROWS, stride=width), :]) for m in range(HALF)]
-        res = [par_ref[pl.ds(base + modes + first + m, ROWS, stride=width), :] for m in range(HALF)]
-        start = tuple(in_ref[first + m] for m in range(HALF))
+        lam = [jnp.exp(-par_ref[tile_rows(group, first + m, stride), :]) for m in range(HALF)]
+        res = [par_ref[tile_rows(group, modes + first + m, stride), :] for m in range(HALF)]
+        start = tuple(in_ref[(first + m) // share, (first + m) % share] for m in range(HALF))
         for m in range(HALF):
             states[0, m] = start[m]
 
@@ -130,12 +237,14 @@
         zeros = tuple(jnp.zeros((ROWS, LANES), jnp.float32) for _ in range(HALF))
         _, sums, skip_sum = lax.fori_loop(0, blocks, forward_body, (start, zeros, skip_sum))
         for m in range(HALF):
-            grad_ref[modes + first + m] = sums[m]
-        incoming = tuple(in_ref[modes + first + m] for m in range(HALF))
+            grad_ref[tile_rows(group, modes + first + m, stride), :] = sums[m]
+        incoming = tuple(in_ref[(first + m) // share, share + (first + m) % share] for m in range(HALF))
         _, sums = lax.fori_loop(0, blocks, backward_body, (incoming, zeros))
         for m in range(HALF):
-            grad_ref[first + m] = -res[m] * sums[m]
-    grad_ref[2 * modes] = skip_sum
+            grad_ref[tile_rows(group, first + m, stride), :] = -res[m] * sums[m]
+    grad_ref[tile_rows(group, 2 * modes, stride), :] = skip_sum
+    for row in range(2 * modes + 1, WIDTH):
+        grad_ref[tile_rows(group, row, stride), :] = jnp.zeros((ROWS, LANES), jnp.float32)
 
     for i in range(ROWS):
         cols = pl.ds(i * LANES, LANES)
@@ -148,48 +257,72 @@
         gv_ref[:, cols] = (g * k_ref[:, cols].astype(jnp.float32)).astype(jnp.bfloat16)
 
 
-def join_kernel(weight_ref, par_ref, all_ref, out_ref, *, modes, tokens):
+def join_kernel(weight_ref, par_ref, all_ref, out_ref, *, modes, tokens, stride, share):
     count = all_ref.shape[0]
     mine = lax.axis_index("ctx")
-    width = 2 * modes + 1
-    base = pl.program_id(0) * ROWS * width
+    group = pl.program_id(0)
     for m in range(modes):
-        across = jnp.exp(-float(tokens) * par_ref[pl.ds(base + m, ROWS, stride=width), :])
+        across = jnp.exp(-float(tokens) * par_ref[tile_rows(group, m, stride), :])
 
         def turn(i, carry):
             state, adjoint = carry
             j = count - 1 - i
-            near = across * weight_ref[i] * state + all_ref[i, m]
-            far = across * weight_ref[j] * adjoint + all_ref[j, modes + m]
+            near = across * weight_ref[i] * state + all_ref[i, m // share, m % share]
+            far = across * weight_ref[j] * adjoint + all_ref[j, m // share, share + m % share]
             state = jnp.where(i < mine, near, state)
             adjoint = jnp.where(j > mine, far, adjoint)
             return state, adjoint
 
         zero = jnp.zeros((ROWS, LANES), jnp.float32)
         state, adjoint = lax.fori_loop(0, count, turn, (zero, zero), unroll=8)
-        out_ref[m] = state
-        out_ref[modes + m] = adjoint
+        out_ref[m // share, m % share] = state
+        out_ref[m // share, share + m % share] = adjoint
 
 
 def per_device(hyena_q, hyena_k, hyena_v, hyena_cot, doc_lengths, decay_rate, residues, skip_gain):
     tokens, channels = hyena_q.shape[1], hyena_q.shape[2]
     modes, own = decay_rate.shape
-    width = 2 * modes + 1
     tiles = channels // LANES
     groups = channels // GROUP
     blocks = tokens // ROWS
     pitch = tokens + PAD
     count, mine = lax.axis_size("ctx"), lax.axis_index("ctx")
+    planes = lax.axis_size("dp")
     axes = ("dp", "ctx")
-
-    packed = jnp.concatenate([decay_rate, residues, skip_gain[None, :]], axis=0)
-    params = lax.all_gather(packed, axes, axis=0)
-    if own != LANES:
-        params = params.transpose(1, 0, 2).reshape(width, tiles, LANES).transpose(1, 0, 2)
-    params = params.reshape(tiles * width, LANES)
+    direct = own == LANES and count == ROWS and modes % count == 0 and planes == groups
+    stride = planes * WIDTH if direct else WIDTH
+    share = modes // count if direct else 2
+    tall = 2 * share
+    vmem = pl.BlockSpec(memory_space=pltpu.VMEM)
+    smem = pl.BlockSpec(memory_space=pltpu.SMEM)
+
+    def remote(collective):
+        return pltpu.CompilerParams(
+            collective_id=collective, has_side_effects=True, vmem_limit_bytes=VMEM_LIMIT
+        )
+
+    spare = jnp.zeros((WIDTH - 2 * modes - 1, own), jnp.float32)
+    packed = jnp.concatenate([decay_rate, residues, skip_gain[None, :], spare], axis=0)
+    if direct:
+        params = pl.pallas_call(
+            functools.partial(gather_kernel, planes=planes, count=count),
+            in_specs=[vmem],
+            out_specs=vmem,
+            out_shape=jax.ShapeDtypeStruct((tiles * WIDTH, LANES), jnp.float32),
+            scratch_shapes=[pltpu.SemaphoreType.DMA((planes - 1,))] * 2
+            + [pltpu.SemaphoreType.DMA((count - 1,))] * 2,
+            compiler_params=remote(0),
+            name="gather",
+        )(packed)
+    else:
+        params = lax.all_gather(packed, axes, axis=1, tiled=True)
+        params = params.reshape(WIDTH, tiles, LANES).transpose(1, 0, 2).reshape(tiles * WIDTH, LANES)
 
     lengths = doc_lengths[0]
-    starts = (jnp.cumsum(lengths) - lengths)[1:]
+    ends_of = [lengths[0]]
+    for i in range(1, lengths.shape[0] - 1):
+        ends_of.append(ends_of[-1] + lengths[i])
+    starts = jnp.stack(ends_of)
     position = mine * tokens + jnp.arange(tokens, dtype=jnp.int32)
     starting = jnp.any(position[:, None] == starts[None, :], axis=1)
     keep = jnp.where(starting, 0.0, 1.0).astype(jnp.float32)
@@ -197,53 +330,82 @@
     place = jnp.arange(count)
     closed = jnp.any((starts // tokens)[None, :] == place[:, None], axis=1)
     opened = 1.0 - closed.astype(jnp.float32)
-    weights = opened
     q, k, v, c = hyena_q[0], hyena_k[0], hyena_v[0], hyena_cot[0]
 
-    smem = pl.BlockSpec(memory_space=pltpu.SMEM)
-    whole = pl.BlockSpec((tiles * width, LANES), lambda g: (0, 0))
+    whole = pl.BlockSpec((tiles * WIDTH, LANES), lambda g: (0, 0))
     block = pl.BlockSpec((tokens, GROUP), lambda g: (0, g))
     wide = pltpu.VMEM((ROWS * pitch, LANES), jnp.float32)
-    limit = pltpu.CompilerParams(vmem_limit_bytes=48 * 1024 * 1024)
+    limit = pltpu.CompilerParams(vmem_limit_bytes=VMEM_LIMIT)
 
     def rows_of(n):
-        return pl.BlockSpec((n, ROWS, LANES), lambda g: (0, g, 0))
+        return pl.BlockSpec((n // tall, tall, ROWS, LANES), lambda g: (0, 0, g, 0))
 
     ends = pl.pallas_call(
-        functools.partial(ends_kernel, modes=modes, pitch=pitch),
+        functools.partial(ends_kernel, modes=modes, pitch=pitch, stride=stride, share=share),
         grid=(groups,),
         in_specs=[smem, smem, whole, block, block, block, block],
         out_specs=rows_of(2 * modes),
-        out_shape=jax.ShapeDtypeStruct((2 * modes, tiles, LANES), jnp.float32),
+        out_shape=jax.ShapeDtypeStruct((2 * modes // tall, tall, tiles, LANES), jnp.float32),
         scratch_shapes=[wide, wide],
         compiler_params=limit,
         name="ends",
     )(keep, flags, params, k, v, c, q)
-    everyone = lax.all_gather(ends, "ctx", axis=0)
-    incoming = pl.pallas_call(
-        functools.partial(join_kernel, modes=modes, tokens=tokens),
-        grid=(groups,),
-        in_specs=[smem, whole, pl.BlockSpec((count, 2 * modes, ROWS, LANES), lambda g: (0, 0, g, 0))],
-        out_specs=rows_of(2 * modes),
-        out_shape=jax.ShapeDtypeStruct((2 * modes, tiles, LANES), jnp.float32),
-        compiler_params=limit,
-        name="join",
-    )(weights, params, everyone)
+    if direct:
+        part = pltpu.VMEM((count, tall, tiles, LANES), jnp.float32)
+        incoming = pl.pallas_call(
+            functools.partial(exchange_kernel, planes=planes, count=count, tokens=tokens),
+            in_specs=[smem, vmem, vmem],
+            out_specs=vmem,
+            out_shape=jax.ShapeDtypeStruct(ends.shape, jnp.float32),
+            scratch_shapes=[part, part] + [pltpu.SemaphoreType.DMA((count - 1,))] * 4,
+            compiler_params=remote(1),
+            name="exchange",
+        )(opened, params, ends)
+    else:
+        everyone = lax.all_gather(ends, "ctx", axis=0)
+        incoming = pl.pallas_call(
+            functools.partial(join_kernel, modes=modes, tokens=tokens, stride=stride, share=share),
+            grid=(groups,),
+            in_specs=[
+                smem, whole,
+                pl.BlockSpec((count, 2 * modes // tall, tall, ROWS, LANES), lambda g: (0, 0, 0, g, 0)),
+            ],
+            out_specs=rows_of(2 * modes),
+            out_shape=jax.ShapeDtypeStruct(ends.shape, jnp.float32),
+            compiler_params=limit,
+            name="join",
+        )(opened, params, everyone)
     big = jax.ShapeDtypeStruct((tokens, channels), jnp.bfloat16)
     hyena_out, grad_q, grad_k, grad_v, grads = pl.pallas_call(
-        functools.partial(main_kernel, modes=modes, pitch=pitch),
+        functools.partial(main_kernel, modes=modes, pitch=pitch, stride=stride, share=share),
         grid=(groups,),
         in_specs=[smem, smem, whole, rows_of(2 * modes), block, block, block, block],
-        out_specs=[block, block, block, block, rows_of(width)],
-        out_shape=[big, big, big, big, jax.ShapeDtypeStruct((width, tiles, LANES), jnp.float32)],
+        out_specs=[block, block, block, block, whole],
+        out_shape=[big, big, big, big, jax.ShapeDtypeStruct((tiles * WIDTH, LANES), jnp.float32)],
         scratch_shapes=[wide, wide, wide, wide, pltpu.VMEM((tokens + 1, HALF, ROWS, LANES), jnp.float32)],
         compiler_params=limit,
         name="main",
     )(keep, flags, params, incoming, k, v, c, q)
-    if own == LANES:
-        shared = lax.psum_scatter(grads, axes, scatter_dimension=1, tiled=True).reshape(width, own)
+    if direct:
+        chunk = planes * WIDTH
+        shared = pl.pallas_call(
+            functools.partial(reduce_kernel, planes=planes, count=count),
+            in_specs=[vmem],
+            out_specs=vmem,
+            out_shape=jax.ShapeDtypeStruct((WIDTH, LANES), jnp.float32),
+            scratch_shapes=[
+                pltpu.VMEM((count - 1, chunk, LANES), jnp.float32),
+                pltpu.VMEM((planes, WIDTH, LANES), jnp.float32),
+                pltpu.VMEM((planes - 1, WIDTH, LANES), jnp.float32),
+            ]
+            + [pltpu.SemaphoreType.DMA((count - 1,))] * 2
+            + [pltpu.SemaphoreType.DMA((planes - 1,))] * 2,
+            compiler_params=remote(2),
+            name="reduce",
+        )(grads.reshape(count, chunk, LANES))
     else:
-        shared = lax.psum_scatter(grads.reshape(width, channels), axes, scatter_dimension=1, tiled=True)
+        grads = grads.reshape(tiles, WIDTH, LANES).transpose(1, 0, 2).reshape(WIDTH, channels)
+        shared = lax.psum_scatter(grads, axes, scatter_dimension=1, tiled=True)
     return (
         hyena_out[None], grad_q[None], grad_k[None], grad_v[None],
         shared[:modes], shared[modes : 2 * modes], shared[2 * modes],

time: 265 us -> 97.2 us (0.37)
  waiting for transfers between devices: 159 us -> 0 us
  Pallas kernels: 33.5 us -> 86.8 us
  blocking collectives: 45 us -> 0 us
  between operations: 14.1 us -> 2.66 us
  local copies, waits for them, and re-layouts: 9.91 us -> 3.99 us
    unnamed x3 -> x0, waiting for transfers between devices: 127 us -> none
    pallas_call x3 -> x5, Pallas kernels: 33.5 us -> 86.8 us  [the longest x1 24.7 us: per_device(): pl.pallas_call(functools.partial(main_kernel, modes=modes, pitch=pitch, s...]
    all_gather x1 -> x0, blocking collectives: 45 us -> none  [per_device(): params = lax.all_gather(packed, axes, axis=0)]
    all_gather x1 -> x0, waiting for transfers between devices: 32.6 us -> none  [per_device(): everyone = lax.all_gather(ends, 'ctx', axis=0)]
    unnamed x19 -> x8, local copies, waits for them, and re-layouts: 7.14 us -> 0.73 us
  transfers between devices with their start and end apart: 2 -> 0, of which waited for: 2 -> 0; matrix products, arithmetic and copies ran while one was open for 0% -> 0% of each run, Pallas kernels for 0% -> 0%
where the time goes in v1:
time: 97.2 us; the launch traced here: 96.7 us
  Pallas kernels  86.8 us (89%)
  local copies, waits for them, and re-layouts  3.99 us (4%)
  other arithmetic  3.25 us (3%)
  between operations  2.66 us (3%)
    pallas_call x1, Pallas kernels, per_device(): pl.pallas_call(functools.partial(main_kernel, modes=modes, pitch=pitch, s...  24.7 us
    pallas_call x1, Pallas kernels, per_device(): pl.pallas_call(functools.partial(exchange_kernel, planes=planes, count=co...  18.9 us
    pallas_call x1, Pallas kernels, per_device(): pl.pallas_call(functools.partial(gather_kernel, planes=planes, count=coun...  17.9 us
    pallas_call x1, Pallas kernels, per_device(): pl.pallas_call(functools.partial(reduce_kernel, planes=planes, count=coun...  16.2 us
    pallas_call x1, Pallas kernels, per_device(): pl.pallas_call(functools.partial(ends_kernel, modes=modes, pitch=pitch, s...  9.08 us

profile of v1, /device:TPU:0, one launch (start us, length us, event | category | flops | bytes accessed | tf_op | source)
XLA Modules:
  0.0 96.7 jit_solution(10569921381910054252)
XLA Ops:
  0.7 0.0 copy-start.2
  0.7 0.1 pad.3.clone
  0.7 0.6 copy-done.2
  1.3 0.6 fusion.2
  3.8 0.7 and_select_fusion
  4.6 0.0 copy-start
  4.6 0.0 copy-start.1
  4.6 0.1 compare_reduce_fusion
  4.7 0.1 fusion
  4.8 0.5 convert_subtract_fusion.open_ref
  5.3 0.5 broadcast_select_fusion.keep_ref
  5.8 0.1 reshape.124
  5.9 0.1 reduce_or.28
  6.0 0.0 copy-start.3
  6.0 0.5 convert_element_type.6.flag_ref
  6.5 0.0 copy-done
  6.5 0.0 copy-done.1
  6.5 0.1 copy-done.3
  6.7 0.7 maximum_maximum_fusion.own_ref
  7.4 17.9 %gather.1.par_ref = f32[1280,128]{1,0:T(8,128)} custom-call(f32[40,128]{1,0:T(8,128)} %maximum_maximum_fusion.own_ref), custom_call_target="tpu_custom_call" | custom-call | tf_op jit(solution)/shard_map/gather/pallas_call | solution.py:307
  25.3 9.1 %ends.1.ends_ref = f32[8,4,32,128]{3,2,1,0:T(8,128)} custom-call(f32[128]{0:T(128)} %broadcast_select_fusion.keep_ref, s32[16]{0:T(128)} %convert_element_type.6.flag_ref, f32[1280,128]{1,0:T(8,128)} %gather.1.par_ref, bf16[128,4096]{1,0:T(8,128)(2,1)} %bitcast.15, bf16[128,4096]{1,0:T(8,128)(2,1)} %bitcast.17, bf16[128,4096]{1,0:T(8,128)(2,1)} %bitcast.19, ...), custom_call_target="tpu_custom_call" | custom-call | tf_op jit(solution)/shard_map/ends/pallas_call | solution.py:343
  34.4 18.9 %exchange.1.in_ref = f32[8,4,32,128]{3,2,1,0:T(8,128)} custom-call(f32[8]{0:T(128)} %convert_subtract_fusion.open_ref, f32[1280,128]{1,0:T(8,128)} %gather.1.par_ref, f32[8,4,32,128]{3,2,1,0:T(8,128)} %ends.1.ends_ref), custom_call_target="tpu_custom_call" | custom-call | tf_op jit(solution)/shard_map/exchange/pallas_call | solution.py:355
  53.3 24.7 %main.1 = (bf16[128,4096]{1,0:T(8,128)(2,1)}, bf16[128,4096]{1,0:T(8,128)(2,1)}, bf16[128,4096]{1,0:T(8,128)(2,1)}, bf16[128,4096]{1,0:T(8,128)(2,1)}, f32[1280,128]{1,0:T(8,128)}) custom-call(f32[128]{0:T(128)} %broadcast_select_fusion.keep_ref, s32[16]{0:T(128)} %convert_element_type.6.flag_ref, f32[1280,128]{1,0:T(8,128)} %gather.1.par_ref, ...), custom_call_target="tpu_custom_call" | custom-call | tf_op jit(solution)/shard_map/main/pallas_call | solution.py:379
  77.9 16.2 %reduce.1 = f32[40,128]{1,0:T(8,128)} custom-call(f32[8,160,128]{2,1,0:T(8,128)} %bitcast.23), custom_call_target="tpu_custom_call" | custom-call | tf_op jit(solution)/shard_map/reduce/pallas_call | solution.py:391
  94.2 1.2 %slice_bitcast_fusion = f32[128]{0:T(128)} fusion(f32[40,128]{1,0:T(8,128)} %reduce.1), kind=kLoop, calls=%fused_computation.9 | loop fusion | bytes 1024 | tf_op jit(solution)/shard_map/squeeze | solution.py:411
  95.4 1.3 %fusion.1 = (f32[16,128]{1,0:T(8,128)}, f32[16,128]{1,0:T(8,128)}) fusion(f32[40,128]{1,0:T(8,128)} %reduce.1), kind=kLoop, calls=%fused_computation.13 | loop fusion | bytes 32768 | tf_op jit(solution)/shard_map/slice | solution.py:411
  (2 shorter events, 0.0 us)
Async XLA Ops:
  0.7 0.7 copy-start.2
  4.6 2.0 %copy-start = (f32[16,128]{1,0:T(8,128)S(1)}, f32[16,128]{1,0:T(8,128)}, u32[]{:S(2)}) copy-start(f32[16,128]{1,0:T(8,128)} %param.14) | copy-start | bytes 24580
  4.6 2.0 %copy-start.1 = (f32[16,128]{1,0:T(8,128)S(1)}, f32[16,128]{1,0:T(8,128)}, u32[]{:S(2)}) copy-start(f32[16,128]{1,0:T(8,128)} %param.13) | copy-start | bytes 24580
  6.0 0.7 copy-start.3

commit v2 on v1

v2 whole, which is shorter than its diff:
```python
import functools

import jax
import jax.numpy as jnp
from jax import lax
from jax.experimental import pallas as pl
from jax.experimental.pallas import tpu as pltpu
from jax.sharding import PartitionSpec as P

LANES = 128
ROWS = 8
GROUP = LANES * ROWS
HALF = 8
PAD = 8
WIDTH = 40
VMEM_LIMIT = 56 * 1024 * 1024
MESH = pl.DeviceIdType.MESH


def tile_rows(group, row, stride):
    return pl.ds(group * (ROWS * WIDTH if stride == WIDTH else WIDTH) + row, ROWS, stride=stride)


def greet(peers):
    barrier = pltpu.get_barrier_semaphore()
    for peer in peers:
        pl.semaphore_signal(barrier, inc=1, device_id=peer, device_id_type=MESH)
    pl.semaphore_wait(barrier, len(peers))


def others(axis, size):
    mine = lax.axis_index(axis)
    return [lax.rem(mine + step, size) for step in range(1, size)]


def push(source, target, send, recv, device):
    copy = pltpu.make_async_remote_copy(
        src_ref=source, dst_ref=target, send_sem=send, recv_sem=recv, device_id=device, device_id_type=MESH
    )
    copy.start()
    return copy


def chips_and_sibling(count):
    mine = lax.axis_index("ctx")
    core = lax.rem(mine, 2)
    chip = mine // 2
    chips = count // 2
    peers = [lax.rem(chip + step, chips) for step in range(1, chips)]
    return mine, core, chip, peers, mine + 1 - 2 * core


def opening(lens_ref, first, last):
    start = jnp.int32(0)
    value = jnp.float32(1.0)
    for i in range(lens_ref.shape[1] - 1):
        start = start + lens_ref[0, i]
        value = jnp.where(jnp.logical_and(start >= first, start <= last), jnp.float32(0.0), value)
    return value


def gather_kernel(rate_ref, res_ref, skip_ref, out_ref, send_z, recv_z, send_p, recv_p, send_s, recv_s,
                  *, planes, count):
    zs = others("dp", planes)
    mine, core, chip, peers, sibling = chips_and_sibling(count)
    modes = rate_ref.shape[0]
    greet([{"dp": z} for z in zs] + [{"ctx": 2 * p + core} for p in peers] + [{"ctx": sibling}])

    def bundle(device):
        return pl.ds(pl.multiple_of(device * (planes * WIDTH), WIDTH), planes * WIDTH)

    base = pl.multiple_of((mine * planes + lax.axis_index("dp")) * WIDTH, WIDTH)
    slot = pl.ds(base, WIDTH)
    out_ref[slot, :] = jnp.concatenate(
        [rate_ref[...], res_ref[...], jnp.broadcast_to(skip_ref[...], (WIDTH - 2 * modes, LANES))], axis=0
    )
    copies = [
        push(out_ref.at[slot], out_ref.at[slot], send_z.at[i], recv_z.at[i], {"dp": z}) for i, z in enumerate(zs)
    ]
    for copy in copies:
        copy.wait()
    own = out_ref.at[bundle(mine)]
    far = [push(own, own, send_p.at[i], recv_p.at[i], {"ctx": 2 * p + core}) for i, p in enumerate(peers)]
    near = [push(own, own, send_s.at[0], recv_s.at[0], {"ctx": sibling})]
    chips = len(peers) + 1
    for i, copy in enumerate(far):
        copy.wait_recv()
        got = out_ref.at[bundle(2 * lax.rem(chip + chips - 1 - i, chips) + core)]
        near.append(push(got, got, send_s.at[i + 1], recv_s.at[i + 1], {"ctx": sibling}))
    for copy in far:
        copy.wait_send()
    for copy in near:
        copy.wait()


def exchange_kernel(lens_ref, par_ref, ends_ref, out_ref, pair, total, land, back,
                    send_s, recv_s, send_p, recv_p, *, planes, count, tokens):
    mine, core, chip, peers, sibling = chips_and_sibling(count)
    greet([{"ctx": 2 * p + core} for p in peers] + [{"ctx": sibling}])
    share = ends_ref.shape[1] // 2
    chips = count // 2
    first = push(ends_ref.at[1 - core], pair, send_s.at[0], recv_s.at[0], {"ctx": sibling})
    even_open = opening(lens_ref, 2 * chip * tokens, (2 * chip + 1) * tokens - 1)
    odd_open = opening(lens_ref, (2 * chip + 1) * tokens, (2 * chip + 2) * tokens - 1)
    is_even = core == 0

    def across(m, g):
        rates = par_ref[pl.ds(g * WIDTH + core * share + m, ROWS, stride=planes * WIDTH), :]
        return jnp.exp(-float(tokens) * rates)

    def both(row, rows):
        own, other = ends_ref[core, row, rows, :], pair[row, rows, :]
        return jnp.where(is_even, own, other), jnp.where(is_even, other, own)

    first.wait()

    def join_cores(m, carry):
        for g in range(planes):
            rows = pl.ds(g * ROWS, ROWS)
            factor = across(m, g)
            even, odd = both(m, rows)
            total[0, m, rows, :] = odd + factor * odd_open * even
            even, odd = both(share + m, rows)
            total[1, m, rows, :] = even + factor * even_open * odd
        return carry

    lax.fori_loop(0, share, join_cores, 0)
    copies = [
        push(total.at[jnp.where(p > chip, 0, 1)], land.at[chip], send_p.at[i], recv_p.at[i], {"ctx": 2 * p + core})
        for i, p in enumerate(peers)
    ]
    land[chip] = jnp.zeros(land.shape[1:], jnp.float32)
    opened = [opening(lens_ref, 2 * r * tokens, (2 * r + 2) * tokens - 1) for r in range(chips)]
    for copy in copies:
        copy.wait()

    def enter(m, carry):
        for g in range(planes):
            rows = pl.ds(g * ROWS, ROWS)
            factor = across(m, g)
            square = factor * factor
            state = jnp.zeros((ROWS, LANES), jnp.float32)
            adjoint = state
            for r in range(chips):
                n = chips - 1 - r
                state = jnp.where(r < chip, square * opened[r] * state + land[r, m, rows, :], state)
                adjoint = jnp.where(n > chip, square * opened[n] * adjoint + land[n, m, rows, :], adjoint)
            even_tail, _ = both(m, rows)
            _, odd_head = both(share + m, rows)
            odd_state = even_tail + factor * even_open * state
            even_adjoint = odd_head + factor * odd_open * adjoint
            out_ref[core, m, rows, :] = jnp.where(is_even, state, odd_state)
            out_ref[core, share + m, rows, :] = jnp.where(is_even, even_adjoint, adjoint)
            back[m, rows, :] = jnp.where(is_even, odd_state, state)
            back[share + m, rows, :] = jnp.where(is_even, adjoint, even_adjoint)
        return carry

    lax.fori_loop(0, share, enter, 0)
    push(back, out_ref.at[core], send_s.at[1], recv_s.at[1], {"ctx": sibling}).wait()


def reduce_kernel(grad_ref, rate_ref, res_ref, skip_ref, pair, stage, land, bundle, land_z,
                  send_s, recv_s, send_p, recv_p, send_z, recv_z, *, planes, count):
    zs = others("dp", planes)
    mine, core, chip, peers, sibling = chips_and_sibling(count)
    plane = lax.axis_index("dp")
    greet([{"dp": z} for z in zs] + [{"ctx": 2 * p + core} for p in peers] + [{"ctx": sibling}])
    order = peers + [chip]
    near = [
        push(grad_ref.at[2 * p + 1 - core], pair.at[i], send_s.at[i], recv_s.at[i], {"ctx": sibling})
        for i, p in enumerate(order)
    ]
    far = []
    for i, p in enumerate(peers):
        near[i].wait_recv()
        stage[i] = grad_ref[2 * p + core] + pair[i]
        far.append(push(stage.at[i], land.at[i], send_p.at[i], recv_p.at[i], {"ctx": 2 * p + core}))
    last = len(peers)
    near[last].wait_recv()
    for copy in near:
        copy.wait_send()
    for copy in far:
        copy.wait()
    for z in range(planes):
        rows = pl.ds(z * WIDTH, WIDTH)
        total = grad_ref[mine, rows, :] + pair[last, rows, :]
        for i in range(last):
            total = total + land[i, rows, :]
        bundle[z] = total
    copies = [
        push(bundle.at[z], land_z.at[i], send_z.at[i], recv_z.at[i], {"dp": z}) for i, z in enumerate(zs)
    ]
    for copy in copies:
        copy.wait()
    total = bundle[plane]
    for i in range(planes - 1):
        total = total + land_z[i]
    modes = rate_ref.shape[0]
    rate_ref[...] = total[:modes]
    res_ref[...] = total[modes : 2 * modes]
    skip_ref[...] = total[2 * modes : 2 * modes + 1]


def load_products(k_ref, v_ref, c_ref, q_ref, drive, pull, pitch):
    tokens = k_ref.shape[0]
    for i in range(ROWS):
        cols = pl.ds(i * LANES, LANES)
        rows = pl.ds(i * pitch, tokens)
        drive[rows, :] = k_ref[:, cols].astype(jnp.float32) * v_ref[:, cols].astype(jnp.float32)
        pull[rows, :] = c_ref[:, cols].astype(jnp.float32) * q_ref[:, cols].astype(jnp.float32)


def ends_kernel(lens_ref, par_ref, k_ref, v_ref, c_ref, q_ref, out_ref, drive, pull, *, modes, pitch, stride, share):
    tokens = k_ref.shape[0]
    blocks = tokens // ROWS
    group = pl.program_id(0)
    origin = lax.axis_index("ctx") * tokens

    def keep(t):
        return opening(lens_ref, origin + t, origin + t)

    def broken(b):
        return opening(lens_ref, origin + b * ROWS, origin + b * ROWS + ROWS - 1) < 0.5

    load_products(k_ref, v_ref, c_ref, q_ref, drive, pull, pitch)
    lam = [jnp.exp(-par_ref[tile_rows(group, m, stride), :]) for m in range(modes)]

    def steps(b, carry, masked):
        tails, heads = list(carry[0]), list(carry[1])
        for j in range(ROWS):
            t = b * ROWS + j
            u = tokens - 1 - t
            d = drive[pl.ds(t, ROWS, stride=pitch), :]
            p = pull[pl.ds(u, ROWS, stride=pitch), :]
            for m in range(modes):
                if masked:
                    tails[m] = lam[m] * keep(t) * tails[m] + d
                    heads[m] = lam[m] * keep(u) * (heads[m] + p)
                else:
                    tails[m] = lam[m] * tails[m] + d
                    heads[m] = lam[m] * (heads[m] + p)
        return tuple(tails), tuple(heads)

    def body(b, carry):
        either = jnp.logical_or(broken(b), broken(blocks - 1 - b))
        return lax.cond(either, lambda c: steps(b, c, True), lambda c: steps(b, c, False), carry)

    zeros = tuple(jnp.zeros((ROWS, LANES), jnp.float32) for _ in range(modes))
    tails, heads = lax.fori_loop(0, blocks, body, (zeros, zeros))
    for m in range(modes):
        out_ref[m // share, m % share] = tails[m]
        out_ref[m // share, share + m % share] = heads[m]


def main_kernel(
    lens_ref, par_ref, in_ref, k_ref, v_ref, c_ref, q_ref,
    out_ref, gq_ref, gk_ref, gv_ref, grad_ref,
    drive, pull, filt, gdrive, states, *, modes, pitch, stride, share,
):
    tokens = k_ref.shape[0]
    blocks = tokens // ROWS
    group = pl.program_id(0)
    origin = lax.axis_index("ctx") * tokens

    def keep(t):
        return opening(lens_ref, origin + t, origin + t)

    def broken(b):
        return opening(lens_ref, origin + b * ROWS, origin + b * ROWS + ROWS - 1) < 0.5

    load_products(k_ref, v_ref, c_ref, q_ref, drive, pull, pitch)
    skip = par_ref[tile_rows(group, 2 * modes, stride), :]
    skip_sum = jnp.zeros((ROWS, LANES), jnp.float32)

    for first in range(0, modes, HALF):
        lam = [jnp.exp(-par_ref[tile_rows(group, first + m, stride), :]) for m in range(HALF)]
        res = [par_ref[tile_rows(group, modes + first + m, stride), :] for m in range(HALF)]
        start = tuple(in_ref[(first + m) // share, (first + m) % share] for m in range(HALF))
        for m in range(HALF):
            states[0, m] = start[m]

        def forward(b, carry, masked):
            x, sums, skips = list(carry[0]), list(carry[1]), carry[2]
            for j in range(ROWS):
                t = b * ROWS + j
                here = pl.ds(t, ROWS, stride=pitch)
                d = drive[here, :]
                p = pull[here, :]
                if first == 0:
                    total = skip * d
                    skips = skips + p * d
                else:
                    total = filt[here, :]
                for m in range(HALF):
                    if masked:
                        x[m] = lam[m] * keep(t) * x[m] + d
                    else:
                        x[m] = lam[m] * x[m] + d
                    states[t + 1, m] = x[m]
                    sums[m] = sums[m] + p * x[m]
                    total = total + res[m] * x[m]
                filt[here, :] = total
            return tuple(x), tuple(sums), skips

        def backward(b, carry, masked):
            inc, sums = list(carry[0]), list(carry[1])
            for j in reversed(range(ROWS)):
                t = b * ROWS + j
                here = pl.ds(t, ROWS, stride=pitch)
                p = pull[here, :]
                total = skip * p if first == 0 else gdrive[here, :]
                for m in range(HALF):
                    a = p + inc[m]
                    total = total + res[m] * a
                    inc[m] = lam[m] * keep(t) * a if masked else lam[m] * a
                    sums[m] = sums[m] + inc[m] * states[t, m]
                gdrive[here, :] = total
            return tuple(inc), tuple(sums)

        def forward_body(b, carry):
            return lax.cond(
                broken(b), lambda c: forward(b, c, True), lambda c: forward(b, c, False), carry
            )

        def backward_body(i, carry):
            b = blocks - 1 - i
            return lax.cond(
                broken(b), lambda c: backward(b, c, True), lambda c: backward(b, c, False), carry
            )

        zeros = tuple(jnp.zeros((ROWS, LANES), jnp.float32) for _ in range(HALF))
        _, sums, skip_sum = lax.fori_loop(0, blocks, forward_body, (start, zeros, skip_sum))
        for m in range(HALF):
            grad_ref[tile_rows(group, modes + first + m, stride), :] = sums[m]
        incoming = tuple(in_ref[(first + m) // share, share + (first + m) % share] for m in range(HALF))
        _, sums = lax.fori_loop(0, blocks, backward_body, (incoming, zeros))
        for m in range(HALF):
            grad_ref[tile_rows(group, first + m, stride), :] = -res[m] * sums[m]
    grad_ref[tile_rows(group, 2 * modes, stride), :] = skip_sum
    for row in range(2 * modes + 1, WIDTH):
        grad_ref[tile_rows(group, row, stride), :] = jnp.zeros((ROWS, LANES), jnp.float32)

    for i in range(ROWS):
        cols = pl.ds(i * LANES, LANES)
        rows = pl.ds(i * pitch, tokens)
        f = filt[rows, :]
        g = gdrive[rows, :]
        out_ref[:, cols] = (q_ref[:, cols].astype(jnp.float32) * f).astype(jnp.bfloat16)
        gq_ref[:, cols] = (c_ref[:, cols].astype(jnp.float32) * f).astype(jnp.bfloat16)
        gk_ref[:, cols] = (g * v_ref[:, cols].astype(jnp.float32)).astype(jnp.bfloat16)
        gv_ref[:, cols] = (g * k_ref[:, cols].astype(jnp.float32)).astype(jnp.bfloat16)


def join_kernel(lens_ref, par_ref, all_ref, out_ref, *, modes, tokens, stride, share):
    count = all_ref.shape[0]
    mine = lax.axis_index("ctx")
    group = pl.program_id(0)
    for m in range(modes):
        across = jnp.exp(-float(tokens) * par_ref[tile_rows(group, m, stride), :])

        def turn(i, carry):
            state, adjoint = carry
            j = count - 1 - i
            near = across * opening(lens_ref, i * tokens, (i + 1) * tokens - 1) * state + all_ref[i, m // share, m % share]
            far = across * opening(lens_ref, j * tokens, (j + 1) * tokens - 1) * adjoint + all_ref[j, m // share, share + m % share]
            state = jnp.where(i < mine, near, state)
            adjoint = jnp.where(j > mine, far, adjoint)
            return state, adjoint

        zero = jnp.zeros((ROWS, LANES), jnp.float32)
        state, adjoint = lax.fori_loop(0, count, turn, (zero, zero), unroll=8)
        out_ref[m // share, m % share] = state
        out_ref[m // share, share + m % share] = adjoint


def per_device(hyena_q, hyena_k, hyena_v, hyena_cot, doc_lengths, decay_rate, residues, skip_gain):
    tokens, channels = hyena_q.shape[1], hyena_q.shape[2]
    modes, own = decay_rate.shape
    tiles = channels // LANES
    groups = channels // GROUP
    pitch = tokens + PAD
    count = lax.axis_size("ctx")
    planes = lax.axis_size("dp")
    axes = ("dp", "ctx")
    direct = own == LANES and count == ROWS and modes % 2 == 0 and planes == groups
    stride = planes * WIDTH if direct else WIDTH
    share = modes // 2
    tall = 2 * share
    vmem = pl.BlockSpec(memory_space=pltpu.VMEM)
    smem = pl.BlockSpec(memory_space=pltpu.SMEM)

    def remote(collective):
        return pltpu.CompilerParams(
            collective_id=collective, has_side_effects=True, vmem_limit_bytes=VMEM_LIMIT
        )

    if direct:
        params = pl.pallas_call(
            functools.partial(gather_kernel, planes=planes, count=count),
            in_specs=[vmem, vmem, vmem],
            out_specs=vmem,
            out_shape=jax.ShapeDtypeStruct((tiles * WIDTH, LANES), jnp.float32),
            scratch_shapes=[pltpu.SemaphoreType.DMA((planes - 1,))] * 2
            + [pltpu.SemaphoreType.DMA((count // 2 - 1,))] * 2
            + [pltpu.SemaphoreType.DMA((count // 2,))] * 2,
            compiler_params=remote(0),
            name="gather",
        )(decay_rate, residues, skip_gain[None, :])
    else:
        spare = jnp.zeros((WIDTH - 2 * modes - 1, own), jnp.float32)
        packed = jnp.concatenate([decay_rate, residues, skip_gain[None, :], spare], axis=0)
        params = lax.all_gather(packed, axes, axis=1, tiled=True)
        params = params.reshape(WIDTH, tiles, LANES).transpose(1, 0, 2).reshape(tiles * WIDTH, LANES)

    q, k, v, c = hyena_q[0], hyena_k[0], hyena_v[0], hyena_cot[0]

    whole = pl.BlockSpec((tiles * WIDTH, LANES), lambda g: (0, 0))
    block = pl.BlockSpec((tokens, GROUP), lambda g: (0, g))
    wide = pltpu.VMEM((ROWS * pitch, LANES), jnp.float32)
    limit = pltpu.CompilerParams(vmem_limit_bytes=VMEM_LIMIT)

    def rows_of(n):
        return pl.BlockSpec((n // tall, tall, ROWS, LANES), lambda g: (0, 0, g, 0))

    ends = pl.pallas_call(
        functools.partial(ends_kernel, modes=modes, pitch=pitch, stride=stride, share=share),
        grid=(groups,),
        in_specs=[smem, whole, block, block, block, block],
        out_specs=rows_of(2 * modes),
        out_shape=jax.ShapeDtypeStruct((2 * modes // tall, tall, tiles, LANES), jnp.float32),
        scratch_shapes=[wide, wide],
        compiler_params=limit,
        name="ends",
    )(doc_lengths, params, k, v, c, q)
    if direct:
        part = pltpu.VMEM((tall, tiles, LANES), jnp.float32)
        chips = count // 2
        incoming = pl.pallas_call(
            functools.partial(exchange_kernel, planes=planes, count=count, tokens=tokens),
            in_specs=[smem, vmem, vmem],
            out_specs=vmem,
            out_shape=jax.ShapeDtypeStruct(ends.shape, jnp.float32),
            scratch_shapes=[
                part,
                pltpu.VMEM((2, share, tiles, LANES), jnp.float32),
                pltpu.VMEM((chips, share, tiles, LANES), jnp.float32),
                part,
            ]
            + [pltpu.SemaphoreType.DMA((2,))] * 2
            + [pltpu.SemaphoreType.DMA((chips - 1,))] * 2,
            compiler_params=remote(1),
            name="exchange",
        )(doc_lengths, params, ends)
    else:
        everyone = lax.all_gather(ends, "ctx", axis=0)
        incoming = pl.pallas_call(
            functools.partial(join_kernel, modes=modes, tokens=tokens, stride=stride, share=share),
            grid=(groups,),
            in_specs=[
                smem, whole,
                pl.BlockSpec((count, 2 * modes // tall, tall, ROWS, LANES), lambda g: (0, 0, 0, g, 0)),
            ],
            out_specs=rows_of(2 * modes),
            out_shape=jax.ShapeDtypeStruct(ends.shape, jnp.float32),
            compiler_params=limit,
            name="join",
        )(doc_lengths, params, everyone)
    big = jax.ShapeDtypeStruct((tokens, channels), jnp.bfloat16)
    hyena_out, grad_q, grad_k, grad_v, grads = pl.pallas_call(
        functools.partial(main_kernel, modes=modes, pitch=pitch, stride=stride, share=share),
        grid=(groups,),
        in_specs=[smem, whole, rows_of(2 * modes), block, block, block, block],
        out_specs=[block, block, block, block, whole],
        out_shape=[big, big, big, big, jax.ShapeDtypeStruct((tiles * WIDTH, LANES), jnp.float32)],
        scratch_shapes=[wide, wide, wide, wide, pltpu.VMEM((tokens + 1, HALF, ROWS, LANES), jnp.float32)],
        compiler_params=limit,
        name="main",
    )(doc_lengths, params, incoming, k, v, c, q)
    if direct:
        chunk = planes * WIDTH
        row = jax.ShapeDtypeStruct((modes, LANES), jnp.float32)
        grad_rate, grad_residues, grad_skip = pl.pallas_call(
            functools.partial(reduce_kernel, planes=planes, count=count),
            in_specs=[vmem],
            out_specs=[vmem, vmem, vmem],
            out_shape=[row, row, jax.ShapeDtypeStruct((1, LANES), jnp.float32)],
            scratch_shapes=[
                pltpu.VMEM((chips, chunk, LANES), jnp.float32),
                pltpu.VMEM((chips - 1, chunk, LANES), jnp.float32),
                pltpu.VMEM((chips - 1, chunk, LANES), jnp.float32),
                pltpu.VMEM((planes, WIDTH, LANES), jnp.float32),
                pltpu.VMEM((planes - 1, WIDTH, LANES), jnp.float32),
            ]
            + [pltpu.SemaphoreType.DMA((chips,))] * 2
            + [pltpu.SemaphoreType.DMA((chips - 1,))] * 2
            + [pltpu.SemaphoreType.DMA((planes - 1,))] * 2,
            compiler_params=remote(2),
            name="reduce",
        )(grads.reshape(count, chunk, LANES))
        grad_skip = grad_skip[0]
    else:
        grads = grads.reshape(tiles, WIDTH, LANES).transpose(1, 0, 2).reshape(WIDTH, channels)
        shared = lax.psum_scatter(grads, axes, scatter_dimension=1, tiled=True)
        grad_rate, grad_residues, grad_skip = shared[:modes], shared[modes : 2 * modes], shared[2 * modes]
    return (
        hyena_out[None], grad_q[None], grad_k[None], grad_v[None],
        grad_rate, grad_residues, grad_skip,
    )


def solution(mesh):
    tokens_split = P("dp", "ctx", None)
    by_channel = P(None, ("dp", "ctx"))
    return jax.shard_map(
        per_device,
        mesh=mesh,
        in_specs=(tokens_split,) * 4 + (P("dp", None), by_channel, by_channel, P(("dp", "ctx"))),
        out_specs=(tokens_split,) * 4 + (by_channel, by_channel, P(("dp", "ctx"))),
        check_vma=False,
    )
```

time: 97.2 us -> 85.2 us (0.88)
  Pallas kernels: 86.8 us -> 81.8 us
  other arithmetic: 3.25 us -> 0 us
  between operations: 2.66 us -> 0.67 us
  local copies, waits for them, and re-layouts: 3.99 us -> 2.48 us
    pallas_call x1, Pallas kernels: 18.9 us -> 14.6 us  [per_device(): pl.pallas_call(functools.partial(exchange_kernel, planes=planes, count=co...]
    pallas_call x1, Pallas kernels: 17.9 us -> 15.9 us  [per_device(): pl.pallas_call(functools.partial(gather_kernel, planes=planes, count=coun...]
    slice x2 -> x0, local copies, waits for them, and re-layouts: 1.9 us -> none  [the longest x1 1.32 us: per_device(): shared[modes:2 * modes]]
    unnamed x8 -> x7, local copies, waits for them, and re-layouts: 0.73 us -> 2.48 us
    pallas_call x1, Pallas kernels: 24.7 us -> 26.3 us  [per_device(): pl.pallas_call(functools.partial(main_kernel, modes=modes, pitch=pitch, s...]
    select_n x2 -> x0, other arithmetic: 1.24 us -> none  [the longest x1 0.73 us: per_device(): closed = jnp.any((starts // tokens)[None, :] == place[:, None], axis=1)]
    squeeze x1 -> x0, local copies, waits for them, and re-layouts: 1.19 us -> none  [per_device(): shared[2 * modes]]
    pallas_call x1, Pallas kernels: 16.2 us -> 15.2 us  [per_device(): pl.pallas_call(functools.partial(reduce_kernel, planes=planes, count=coun...]
where the time goes in v2:
time: 85.2 us; the launch traced here: 84.9 us
  Pallas kernels  81.8 us (96%)
  local copies, waits for them, and re-layouts  2.48 us (3%)
    pallas_call x1, Pallas kernels, per_device(): pl.pallas_call(functools.partial(main_kernel, modes=modes, pitch=pitch, s...  26.3 us
    pallas_call x1, Pallas kernels, per_device(): pl.pallas_call(functools.partial(gather_kernel, planes=planes, count=coun...  15.9 us
    pallas_call x1, Pallas kernels, per_device(): pl.pallas_call(functools.partial(reduce_kernel, planes=planes, count=coun...  15.2 us
    pallas_call x1, Pallas kernels, per_device(): pl.pallas_call(functools.partial(exchange_kernel, planes=planes, count=co...  14.6 us
    pallas_call x1, Pallas kernels, per_device(): pl.pallas_call(functools.partial(ends_kernel, modes=modes, pitch=pitch, s...  9.8 us
    unnamed x7, local copies, waits for them, and re-layouts  2.48 us

profile of v2, /device:TPU:0, one launch (start us, length us, event | category | flops | bytes accessed | tf_op | source)
XLA Modules:
  0.0 84.9 jit_solution(1212436841941551591)
XLA Ops:
  0.6 15.9 %gather.1.par_ref = f32[1280,128]{1,0:T(8,128)} custom-call(f32[16,128]{1,0:T(8,128)} %rate_ref.1, f32[16,128]{1,0:T(8,128)} %res_ref.1, f32[1,128]{1,0:T(1,128)} %bitcast.20), custom_call_target="tpu_custom_call" | custom-call | tf_op jit(solution)/shard_map/gather/pallas_call | solution.py:398
  16.5 9.8 %ends.1.ends_ref = f32[2,16,32,128]{3,2,1,0:T(8,128)} custom-call(s32[1,4]{1,0:T(1,128)} %lens_ref.5, f32[1280,128]{1,0:T(8,128)} %gather.1.par_ref, bf16[128,4096]{1,0:T(8,128)(2,1)} %bitcast.11, bf16[128,4096]{1,0:T(8,128)(2,1)} %bitcast.13, bf16[128,4096]{1,0:T(8,128)(2,1)} %bitcast.15, bf16[128,4096]{1,0:T(8,128)(2,1)} %bitcast.17), custom_call_target="tpu_custom_call" | custom-call | tf_op jit(solution)/shard_map/ends/pallas_call | solution.py:425
  26.3 14.6 %exchange.1.in_ref = f32[2,16,32,128]{3,2,1,0:T(8,128)} custom-call(s32[1,4]{1,0:T(1,128)} %lens_ref.5, f32[1280,128]{1,0:T(8,128)} %gather.1.par_ref, f32[2,16,32,128]{3,2,1,0:T(8,128)} %ends.1.ends_ref), custom_call_target="tpu_custom_call" | custom-call | tf_op jit(solution)/shard_map/exchange/pallas_call | solution.py:438
  40.9 26.3 %main.1 = (bf16[128,4096]{1,0:T(8,128)(2,1)}, bf16[128,4096]{1,0:T(8,128)(2,1)}, bf16[128,4096]{1,0:T(8,128)(2,1)}, bf16[128,4096]{1,0:T(8,128)(2,1)}, f32[1280,128]{1,0:T(8,128)}) custom-call(s32[1,4]{1,0:T(1,128)} %lens_ref.5, f32[1280,128]{1,0:T(8,128)} %gather.1.par_ref, f32[2,16,32,128]{3,2,1,0:T(8,128)} %exchange.1.in_ref, bf16[128,4096]{1,0:T(8,128)(2,1)} %bitcast.12, ...), custom_call_target="tpu_custom_call" | custom-call | tf_op jit(solution)/shard_map/main/pallas_call | solution.py:469
  67.2 15.2 %reduce.1 = (f32[16,128]{1,0:T(8,128)}, f32[16,128]{1,0:T(8,128)}, f32[1,128]{1,0:T(1,128)}) custom-call(f32[8,160,128]{2,1,0:T(8,128)} %bitcast.19), custom_call_target="tpu_custom_call" | custom-call | tf_op jit(solution)/shard_map/reduce/pallas_call | solution.py:482
  82.4 0.0 copy-start
  82.4 1.3 %copy.18 = f32[16,128]{1,0:T(8,128)} copy(f32[16,128]{1,0:T(8,128)} %get-tuple-element.34) | data formatting | bytes 16384
  83.7 0.0 copy-done
  83.8 0.0 copy-start.1
  83.8 0.6 copy.19
  84.4 0.1 copy-done.1
  84.4 0.5 copy.20
Async XLA Ops:
  82.4 1.3 %copy-start = (f32[16,128]{1,0:T(8,128)S(1)}, f32[16,128]{1,0:T(8,128)}, u32[]{:S(2)}) copy-start(f32[16,128]{1,0:T(8,128)} %get-tuple-element.35) | copy-start | bytes 24580
  83.8 0.7 copy-start.1

commit v3 on v2

--- a/solution.py
+++ b/solution.py
@@ -9,6 +9,7 @@
 
 LANES = 128
 ROWS = 8
+STEP = 16
 GROUP = LANES * ROWS
 HALF = 8
 PAD = 8
@@ -212,7 +213,7 @@
 
 def ends_kernel(lens_ref, par_ref, k_ref, v_ref, c_ref, q_ref, out_ref, drive, pull, *, modes, pitch, stride, share):
     tokens = k_ref.shape[0]
-    blocks = tokens // ROWS
+    blocks = tokens // STEP
     group = pl.program_id(0)
     origin = lax.axis_index("ctx") * tokens
 
@@ -220,15 +221,15 @@
         return opening(lens_ref, origin + t, origin + t)
 
     def broken(b):
-        return opening(lens_ref, origin + b * ROWS, origin + b * ROWS + ROWS - 1) < 0.5
+        return opening(lens_ref, origin + b * STEP, origin + b * STEP + STEP - 1) < 0.5
 
     load_products(k_ref, v_ref, c_ref, q_ref, drive, pull, pitch)
     lam = [jnp.exp(-par_ref[tile_rows(group, m, stride), :]) for m in range(modes)]
 
     def steps(b, carry, masked):
         tails, heads = list(carry[0]), list(carry[1])
-        for j in range(ROWS):
-            t = b * ROWS + j
+        for j in range(STEP):
+            t = b * STEP + j
             u = tokens - 1 - t
             d = drive[pl.ds(t, ROWS, stride=pitch), :]
             p = pull[pl.ds(u, ROWS, stride=pitch), :]
@@ -258,7 +259,7 @@
     drive, pull, filt, gdrive, states, *, modes, pitch, stride, share,
 ):
     tokens = k_ref.shape[0]
-    blocks = tokens // ROWS
+    blocks = tokens // STEP
     group = pl.program_id(0)
     origin = lax.axis_index("ctx") * tokens
 
@@ -266,7 +267,7 @@
         return opening(lens_ref, origin + t, origin + t)
 
     def broken(b):
-        return opening(lens_ref, origin + b * ROWS, origin + b * ROWS + ROWS - 1) < 0.5
+        return opening(lens_ref, origin + b * STEP, origin + b * STEP + STEP - 1) < 0.5
 
     load_products(k_ref, v_ref, c_ref, q_ref, drive, pull, pitch)
     skip = par_ref[tile_rows(group, 2 * modes, stride), :]
@@ -281,8 +282,8 @@
 
         def forward(b, carry, masked):
             x, sums, skips = list(carry[0]), list(carry[1]), carry[2]
-            for j in range(ROWS):
-                t = b * ROWS + j
+            for j in range(STEP):
+                t = b * STEP + j
                 here = pl.ds(t, ROWS, stride=pitch)
                 d = drive[here, :]
                 p = pull[here, :]
@@ -304,8 +305,8 @@
 
         def backward(b, carry, masked):
             inc, sums = list(carry[0]), list(carry[1])
-            for j in reversed(range(ROWS)):
-                t = b * ROWS + j
+            for j in reversed(range(STEP)):
+                t = b * STEP + j
                 here = pl.ds(t, ROWS, stride=pitch)
                 p = pull[here, :]
                 total = skip * p if first == 0 else gdrive[here, :]

time: 85.2 us -> 81.6 us (0.958)
  Pallas kernels: 81.8 us -> 78.4 us
    pallas_call x1, Pallas kernels: 26.3 us -> 22.8 us  [per_device(): pl.pallas_call(functools.partial(main_kernel, modes=modes, pitch=pitch, s...]
    pallas_call x1, Pallas kernels: 9.8 us -> 8.53 us  [per_device(): pl.pallas_call(functools.partial(ends_kernel, modes=modes, pitch=pitch, s...]
    pallas_call x1, Pallas kernels: 14.6 us -> 15.5 us  [per_device(): pl.pallas_call(functools.partial(exchange_kernel, planes=planes, count=co...]
where the time goes in v3:
time: 81.6 us; the launch traced here: 81.5 us
  Pallas kernels  78.4 us (96%)
  local copies, waits for them, and re-layouts  2.48 us (3%)
    pallas_call x1, Pallas kernels, per_device(): pl.pallas_call(functools.partial(main_kernel, modes=modes, pitch=pitch, s...  22.8 us
    pallas_call x1, Pallas kernels, per_device(): pl.pallas_call(functools.partial(gather_kernel, planes=planes, count=coun...  15.9 us
    pallas_call x1, Pallas kernels, per_device(): pl.pallas_call(functools.partial(reduce_kernel, planes=planes, count=coun...  15.7 us
    pallas_call x1, Pallas kernels, per_device(): pl.pallas_call(functools.partial(exchange_kernel, planes=planes, count=co...  15.5 us
    pallas_call x1, Pallas kernels, per_device(): pl.pallas_call(functools.partial(ends_kernel, modes=modes, pitch=pitch, s...  8.53 us
    unnamed x7, local copies, waits for them, and re-layouts  2.48 us

profile of v3, /device:TPU:0, one launch (start us, length us, event | category | flops | bytes accessed | tf_op | source)
XLA Modules:
  0.0 81.5 jit_solution(1663974475069100829)
XLA Ops:
  0.6 15.9 %gather.1.par_ref = f32[1280,128]{1,0:T(8,128)} custom-call(f32[16,128]{1,0:T(8,128)} %rate_ref.1, f32[16,128]{1,0:T(8,128)} %res_ref.1, f32[1,128]{1,0:T(1,128)} %bitcast.20), custom_call_target="tpu_custom_call" | custom-call | tf_op jit(solution)/shard_map/gather/pallas_call | solution.py:399
  16.5 8.5 %ends.1.ends_ref = f32[2,16,32,128]{3,2,1,0:T(8,128)} custom-call(s32[1,4]{1,0:T(1,128)} %lens_ref.5, f32[1280,128]{1,0:T(8,128)} %gather.1.par_ref, bf16[128,4096]{1,0:T(8,128)(2,1)} %bitcast.11, bf16[128,4096]{1,0:T(8,128)(2,1)} %bitcast.13, bf16[128,4096]{1,0:T(8,128)(2,1)} %bitcast.15, bf16[128,4096]{1,0:T(8,128)(2,1)} %bitcast.17), custom_call_target="tpu_custom_call" | custom-call | tf_op jit(solution)/shard_map/ends/pallas_call | solution.py:426
  25.1 15.5 %exchange.1.in_ref = f32[2,16,32,128]{3,2,1,0:T(8,128)} custom-call(s32[1,4]{1,0:T(1,128)} %lens_ref.5, f32[1280,128]{1,0:T(8,128)} %gather.1.par_ref, f32[2,16,32,128]{3,2,1,0:T(8,128)} %ends.1.ends_ref), custom_call_target="tpu_custom_call" | custom-call | tf_op jit(solution)/shard_map/exchange/pallas_call | solution.py:439
  40.6 22.8 %main.1 = (bf16[128,4096]{1,0:T(8,128)(2,1)}, bf16[128,4096]{1,0:T(8,128)(2,1)}, bf16[128,4096]{1,0:T(8,128)(2,1)}, bf16[128,4096]{1,0:T(8,128)(2,1)}, f32[1280,128]{1,0:T(8,128)}) custom-call(s32[1,4]{1,0:T(1,128)} %lens_ref.5, f32[1280,128]{1,0:T(8,128)} %gather.1.par_ref, f32[2,16,32,128]{3,2,1,0:T(8,128)} %exchange.1.in_ref, bf16[128,4096]{1,0:T(8,128)(2,1)} %bitcast.12, ...), custom_call_target="tpu_custom_call" | custom-call | tf_op jit(solution)/shard_map/main/pallas_call | solution.py:470
  63.4 15.7 %reduce.1 = (f32[16,128]{1,0:T(8,128)}, f32[16,128]{1,0:T(8,128)}, f32[1,128]{1,0:T(1,128)}) custom-call(f32[8,160,128]{2,1,0:T(8,128)} %bitcast.19), custom_call_target="tpu_custom_call" | custom-call | tf_op jit(solution)/shard_map/reduce/pallas_call | solution.py:483
  79.0 0.0 copy-start
  79.1 1.3 %copy.18 = f32[16,128]{1,0:T(8,128)} copy(f32[16,128]{1,0:T(8,128)} %get-tuple-element.34) | data formatting | bytes 16384
  80.4 0.0 copy-done
  80.4 0.0 copy-start.1
  80.4 0.6 copy.19
  81.0 0.1 copy-done.1
  81.0 0.5 copy.20
Async XLA Ops:
  79.0 1.3 %copy-start = (f32[16,128]{1,0:T(8,128)S(1)}, f32[16,128]{1,0:T(8,128)}, u32[]{:S(2)}) copy-start(f32[16,128]{1,0:T(8,128)} %get-tuple-element.35) | copy-start | bytes 24580
  80.4 0.7 copy-start.1
